TPU v7x, 32 devices: a whole 2x2x4 slice. The times are simulated.
32 devices in a mesh: dp: 4 (over y, x), tile: 8 (over z, core).
Axes of the slice: x: 2, y: 2, z: 4, core: 2. Of those that a mesh axis runs over, the one named last changes fastest.
Arguments:
- features: bfloat16 [4, 64, 64, 128], P('dp', None, 'tile'), may hold values from -6 to 6
- occupied_block_mask: int32 [4, 8, 2], P('dp', 'tile'), may hold values 0 or 1
- conv_one: bfloat16 [27, 64, 64], replicated, may hold values from -0.15625 to 0.15625
- conv_two: bfloat16 [27, 64, 64], replicated, may hold values from -0.15625 to 0.15625
- gain: float32 [64], replicated, may hold values from 0.5 to 1.5
- shift: float32 [64], replicated, may hold values from -3 to 3
- cotangent: bfloat16 [4, 64, 64, 128], P('dp', None, 'tile'), may hold values from -6 to 6
Outputs:
- section_out: bfloat16 [4, 64, 64, 128], P('dp', None, 'tile')
- input_grad: bfloat16 [4, 64, 64, 128], P('dp', None, 'tile')
- grad_one: float32 [27, 64, 64], replicated
- grad_two: float32 [27, 64, 64], replicated
- gain_grad: float32 [64], replicated
- shift_grad: float32 [64], replicated
Inputs may be any that keep to these rules, and one draw needn't show every extreme that they name: `occupied_block_mask`: each entry marks whether a block holds points.
All inputs are finite; a program needn't handle non-finite values.
Results may differ from a plain program's by a relative error of at most 0.0034.
Values may be sent and summed in bfloat16 or wider, within the bound.
A program may use at most 128 MiB of HBM per device.

v0:
```python
import functools

import jax
import jax.numpy as jnp
from jax import lax
from jax.experimental import pallas as pl
from jax.experimental.pallas import tpu as pltpu
from jax.sharding import PartitionSpec as P

BLK = 8
LANES = 128
EPSILON = 1e-05
MESH = pl.DeviceIdType.MESH
F32 = jnp.float32
BF16 = jnp.bfloat16


def kernel(
    n_dp, n_tile, ch, nx, hy,
    xd_ref, mask_ref, w1_ref, w2_ref, w1f_ref, w2f_ref, gs_ref,
    so_ref, ig_ref, g1_ref, g2_ref, gain_out, shift_out,
    xd_pad, a_pad, i_pad, s_x, s_t, d3, ar_a, ar_b, part, r1, acc, r2, q3, q4,
    halo_s, halo_r, ar_s, ar_r, rs_s, rs_r,
):
    n_a, n_b = 2 * n_dp, n_tile // 2
    dp, tile = lax.axis_index("dp"), lax.axis_index("tile")
    core, z = lax.rem(tile, 2), tile // 2
    a_me = dp * 2 + core
    flat = nx * hy
    c_a = part.shape[1] // n_a
    c_b = c_a // n_b

    def peer_a(k):
        other = lax.rem(a_me + k, n_a)
        return other, (other // 2, z * 2 + lax.rem(other, 2))

    def peer_b(k):
        other = lax.rem(z + k, n_b)
        return other, (dp, other * 2 + core)

    has_left, has_right = tile > 0, tile < n_tile - 1

    barrier = pltpu.get_barrier_semaphore()
    for k in range(1, n_a):
        pl.semaphore_signal(barrier, inc=1, device_id=peer_a(k)[1], device_id_type=MESH)
    for k in range(1, n_b):
        pl.semaphore_signal(barrier, inc=1, device_id=peer_b(k)[1], device_id_type=MESH)

    @pl.when(has_left)
    def _():
        pl.semaphore_signal(barrier, inc=1, device_id=(dp, tile - 1), device_id_type=MESH)

    @pl.when(has_right)
    def _():
        pl.semaphore_signal(barrier, inc=1, device_id=(dp, tile + 1), device_id_type=MESH)

    sides = has_left.astype(jnp.int32) + has_right.astype(jnp.int32)
    pl.semaphore_wait(barrier, n_a + n_b - 2 + sides)

    def halo(phase, src, first, pad):
        low = pltpu.make_async_remote_copy(
            src_ref=src.at[:, pl.ds(first, hy)],
            dst_ref=pad.at[:, pl.ds(flat + hy, hy)],
            send_sem=halo_s.at[phase, 0], recv_sem=halo_r.at[phase, 0],
            device_id=(dp, tile - 1), device_id_type=MESH)
        high = pltpu.make_async_remote_copy(
            src_ref=src.at[:, pl.ds(first + flat - hy, hy)],
            dst_ref=pad.at[:, pl.ds(0, hy)],
            send_sem=halo_s.at[phase, 1], recv_sem=halo_r.at[phase, 1],
            device_id=(dp, tile + 1), device_id_type=MESH)

        @pl.when(has_left)
        def _():
            low.start()

        @pl.when(has_right)
        def _():
            high.start()

        def finish():
            @pl.when(has_left)
            def _():
                low.wait_send()
                high.wait_recv()

            @pl.when(has_right)
            def _():
                high.wait_send()
                low.wait_recv()

        return finish

    def zero_ends(pad):
        @pl.when(jnp.logical_not(has_left))
        def _():
            pad[:, pl.ds(0, hy)] = jnp.zeros((pad.shape[0], hy), pad.dtype)

        @pl.when(jnp.logical_not(has_right))
        def _():
            pad[:, pl.ds(flat + hy, hy)] = jnp.zeros((pad.shape[0], hy), pad.dtype)

    width = hy // BLK
    lane = lax.broadcasted_iota(jnp.int32, (1, hy), 1)
    row_h, row_y = lane // width, lax.rem(lane, width)

    def shifts(pad, first, out):
        def plane(x, carry):
            at = pl.ds(pl.multiple_of(x * hy, hy), hy)
            values = pad[pl.ds(first, ch), at].astype(F32)
            for b in range(3):
                for c in range(3):
                    step = (b - 1) * width + (c - 1)
                    moved = values
                    if step:
                        moved = pltpu.roll(values, (-step) % hy, 1)
                        fits = ((row_h + (b - 1) >= 0) & (row_h + (b - 1) < BLK)
                                & (row_y + (c - 1) >= 0) & (row_y + (c - 1) < width))
                        moved = jnp.where(fits, moved, 0.0)
                    out[pl.ds((3 * b + c) * ch, ch), at] = moved.astype(BF16)
            return carry
        lax.fori_loop(0, nx + 2, plane, 0)

    def conv(weight, stack):
        grown = jnp.dot(weight[...], stack[...], preferred_element_type=F32)
        return (grown[:ch, :flat] + grown[ch:2 * ch, hy:hy + flat]
                + grown[2 * ch:, 2 * hy:2 * hy + flat])

    def kernel_grad(stack, g):
        dims = (((1,), (1,)), ((), ()))
        rows = 9 * ch
        half = rows // 2
        part[g, pl.ds(0, rows), :] = lax.dot_general(
            stack[...], d3[pl.ds(0, 2 * ch), :], dims, preferred_element_type=F32)
        rest = lax.dot_general(
            stack[...], d3[pl.ds(2 * ch, ch), :], dims, preferred_element_type=F32)
        part[g, pl.ds(rows, half), :] = jnp.concatenate([rest[:half], rest[half:]], axis=1)

    def put_d3(value):
        for a in range(3):
            d3[pl.ds(a * ch, ch), pl.ds(a * hy, flat)] = value

    def to_rows(columns):
        spot = lax.broadcasted_iota(jnp.int32, (ch, LANES), 1)
        block = jnp.zeros((ch, LANES), F32)
        for index, column in enumerate(columns):
            block = jnp.where(spot == index, column, block)
        return jnp.transpose(block)[:8]

    def to_columns(rows):
        return jnp.transpose(jnp.concatenate([rows, jnp.zeros((LANES - 8, ch), F32)], axis=0))

    def spread(call, slots, mine, peers, size, base):
        copies = []
        for k in range(1, size):
            copy = pltpu.make_async_remote_copy(
                src_ref=slots.at[call, mine], dst_ref=slots.at[call, mine],
                send_sem=ar_s.at[call, base + k], recv_sem=ar_r.at[call, base + k],
                device_id=peers(k)[1], device_id_type=MESH)
            copy.start()
            copies.append(copy)
        return copies

    def wait_all(copies):
        for copy in copies:
            copy.wait()

    def small_start(call, rows):
        ar_a[call, a_me] = rows
        return spread(call, ar_a, a_me, peer_a, n_a, 0)

    def small_next(call, copies, merge):
        wait_all(copies)
        ar_b[call, z] = merge([ar_a[call, k] for k in range(n_a)])
        return spread(call, ar_b, z, peer_b, n_b, n_a)

    def small_end(call, copies, merge):
        wait_all(copies)
        return merge([ar_b[call, k] for k in range(n_b)])

    def add(rows):
        total = rows[0]
        for row in rows[1:]:
            total = total + row
        return total

    def merge_moments(rows):
        total = add(rows)
        count, sums = total[2:3], total[0:1]
        mean = sums / jnp.maximum(count, 1.0)
        spread_all = total[1:2]
        for row in rows:
            off = row[0:1] / jnp.maximum(row[2:3], 1.0) - mean
            spread_all = spread_all + row[2:3] * off * off
        return jnp.concatenate([sums, spread_all, count, jnp.zeros((5, ch), F32)], axis=0)

    def scatter_a(g):
        copies = []
        for k in range(1, n_a):
            other, device = peer_a(k)
            copy = pltpu.make_async_remote_copy(
                src_ref=part.at[g, pl.ds(pl.multiple_of(other * c_a, c_a), c_a), :],
                dst_ref=r1.at[g, k - 1],
                send_sem=rs_s.at[g, k], recv_sem=rs_r.at[g, k],
                device_id=device, device_id_type=MESH)
            copy.start()
            copies.append(copy)
        return copies

    def scatter_b(g, copies):
        wait_all(copies)
        total = part[g, pl.ds(pl.multiple_of(a_me * c_a, c_a), c_a), :]
        for k in range(1, n_a):
            total = total + r1[g, k - 1]
        acc[g] = total
        copies = []
        for k in range(1, n_b):
            other, device = peer_b(k)
            copy = pltpu.make_async_remote_copy(
                src_ref=acc.at[g, pl.ds(pl.multiple_of(other * c_b, c_b), c_b), :],
                dst_ref=r2.at[g, k - 1],
                send_sem=rs_s.at[g, n_a + k], recv_sem=rs_r.at[g, n_a + k],
                device_id=device, device_id_type=MESH)
            copy.start()
            copies.append(copy)
        return copies

    def gather_b(g, copies):
        wait_all(copies)
        mine = pl.ds(pl.multiple_of(z * c_b, c_b), c_b)
        total = acc[g, mine, :]
        for k in range(1, n_b):
            total = total + r2[g, k - 1]
        q3[g, mine, :] = total.astype(BF16)
        copies = []
        for k in range(1, n_b):
            copy = pltpu.make_async_remote_copy(
                src_ref=q3.at[g, mine, :], dst_ref=q3.at[g, mine, :],
                send_sem=rs_s.at[g, n_a + n_b + k], recv_sem=rs_r.at[g, n_a + n_b + k],
                device_id=peer_b(k)[1], device_id_type=MESH)
            copy.start()
            copies.append(copy)
        return copies

    def gather_a(g, copies):
        wait_all(copies)
        mine = pl.ds(pl.multiple_of(a_me * c_a, c_a), c_a)
        copies = []
        for k in range(1, n_a):
            copy = pltpu.make_async_remote_copy(
                src_ref=q3.at[g], dst_ref=q4.at[g, mine, :],
                send_sem=rs_s.at[g, n_a + 2 * n_b + k], recv_sem=rs_r.at[g, n_a + 2 * n_b + k],
                device_id=peer_a(k)[1], device_id_type=MESH)
            copy.start()
            copies.append(copy)
        q4[g, mine, :] = q3[g]
        return copies

    def write_grad(g, copies, out):
        wait_all(copies)
        rows = 9 * ch
        half = rows // 2
        for a in range(2):
            out[pl.ds(a * rows, rows), :] = q4[g, pl.ds(0, rows), pl.ds(a * ch, ch)].astype(F32)
        for side in range(2):
            out[pl.ds(2 * rows + side * half, half), :] = (
                q4[g, pl.ds(rows, half), pl.ds(side * ch, ch)].astype(F32))

    mask = mask_ref[...]
    end_xd = halo(0, xd_ref, 0, xd_pad)
    xd_pad[:, pl.ds(hy, flat)] = xd_ref[...]
    zero_ends(xd_pad)
    zero_ends(a_pad)
    zero_ends(i_pad)
    d3[...] = jnp.zeros(d3.shape, d3.dtype)
    put_d3(xd_ref[pl.ds(ch, ch), :])
    used = 27 * ch // 2
    for g in range(2):
        part[g, pl.ds(used, part.shape[1] - used), :] = jnp.zeros(
            (part.shape[1] - used, LANES), F32)
    end_xd()

    shifts(xd_pad, 0, s_x)
    pre = conv(w1_ref, s_x)
    count_here = jnp.sum(mask, axis=1, keepdims=True)
    sums_here = jnp.sum(pre * mask, axis=1, keepdims=True)
    off = (pre - sums_here / jnp.maximum(count_here, 1.0)) * mask
    squares_here = jnp.sum(off * off, axis=1, keepdims=True)
    copies = small_start(0, to_rows([sums_here, squares_here, count_here]))

    shifts(xd_pad, ch, s_t)
    act_grad = conv(w2f_ref, s_t)

    copies = small_next(0, copies, merge_moments)
    moments = to_columns(small_end(0, copies, merge_moments))
    count = moments[:, 2:3]
    mean = moments[:, 0:1] / count
    inv_std = lax.rsqrt(moments[:, 1:2] / count + EPSILON)
    gain, shift = gs_ref[:, 0:1], gs_ref[:, 1:2]
    normal = (pre - mean) * inv_std
    pre_act = gain * normal + shift
    sg = 1.0 / (1.0 + jnp.exp(-pre_act))
    a_pad[:, pl.ds(hy, flat)] = (pre_act * sg * mask).astype(BF16)
    end_act = halo(1, a_pad, hy, a_pad)
    z_grad = act_grad * mask * sg * (1.0 + pre_act * (1.0 - sg))
    shift_here = jnp.sum(z_grad, axis=1, keepdims=True)
    gain_here = jnp.sum(z_grad * normal, axis=1, keepdims=True)
    copies = small_start(1, to_rows([shift_here, gain_here]))

    end_act()
    shifts(a_pad, 0, s_t)
    copies = small_next(1, copies, add)
    kernel_grad(s_t, 0)
    totals = small_end(1, copies, add)
    shift_out[...] = totals[0:1]
    gain_out[...] = totals[1:2]
    totals = to_columns(totals)
    delta_one = (gain * inv_std * (
        z_grad - totals[:, 0:1] / count - normal * (totals[:, 1:2] / count)) * mask).astype(BF16)
    i_pad[:, pl.ds(hy, flat)] = delta_one
    end_delta = halo(2, i_pad, hy, i_pad)
    put_d3(delta_one)
    kernel_grad(s_x, 1)
    one = scatter_a(1)
    two = scatter_a(0)
    pre_two = conv(w2_ref, s_t)
    so_ref[...] = ((xd_ref[pl.ds(0, ch), :].astype(F32) + pre_two) * mask).astype(BF16)
    one = scatter_b(1, one)
    end_delta()
    shifts(i_pad, 0, s_t)
    two = scatter_b(0, two)
    one = gather_b(1, one)
    back = conv(w1f_ref, s_t)
    ig_ref[...] = ((xd_ref[pl.ds(ch, ch), :].astype(F32) + back) * mask).astype(BF16)
    two = gather_b(0, two)
    one = gather_a(1, one)
    two = gather_a(0, two)
    write_grad(1, one, g1_ref)
    write_grad(0, two, g2_ref)


def flat_kernel(taps):
    count, inner, outer = taps.shape
    return taps.reshape(3, count // 3 * inner, outer).transpose(0, 2, 1).reshape(3 * outer, -1)


def flat_flipped(taps):
    count, outer, inner = taps.shape
    return (taps[::-1].reshape(3, count // 3, outer, inner).transpose(0, 2, 1, 3)
            .reshape(3 * outer, -1))


def local(n_dp, n_tile, features, occupied, conv_one, conv_two, gain, shift, cotangent):
    scenes, ch, nx, hy = features.shape
    flat = nx * hy
    grown = jnp.broadcast_to(
        occupied[:, :, None, None, :, None],
        (1, nx // BLK, BLK, BLK, occupied.shape[2], BLK)).reshape(1, flat)
    mask = grown.astype(BF16)
    xd = jnp.concatenate(
        [features.reshape(ch, flat), cotangent.reshape(ch, flat)], axis=0) * mask
    n_a, n_b = 2 * n_dp, n_tile // 2
    c_b = -(-(27 * ch // 2) // (n_a * n_b * 16)) * 16
    c_a = c_b * n_b
    rows = c_a * n_a
    vmem = pl.BlockSpec(memory_space=pltpu.VMEM)
    dma = pltpu.SemaphoreType.DMA
    so, ig, g1, g2, gg, sg = pl.pallas_call(
        functools.partial(kernel, n_dp, n_tile, ch, nx, hy),
        out_shape=(
            jax.ShapeDtypeStruct((ch, flat), BF16),
            jax.ShapeDtypeStruct((ch, flat), BF16),
            jax.ShapeDtypeStruct((27 * ch, ch), F32),
            jax.ShapeDtypeStruct((27 * ch, ch), F32),
            jax.ShapeDtypeStruct((1, ch), F32),
            jax.ShapeDtypeStruct((1, ch), F32),
        ),
        in_specs=[vmem] * 7,
        out_specs=[vmem] * 6,
        scratch_shapes=[
            pltpu.VMEM((2 * ch, flat + 2 * hy), BF16),
            pltpu.VMEM((ch, flat + 2 * hy), BF16),
            pltpu.VMEM((ch, flat + 2 * hy), BF16),
            pltpu.VMEM((9 * ch, flat + 2 * hy), BF16),
            pltpu.VMEM((9 * ch, flat + 2 * hy), BF16),
            pltpu.VMEM((3 * ch, flat + 2 * hy), BF16),
            pltpu.VMEM((2, n_a, 8, ch), F32),
            pltpu.VMEM((2, n_b, 8, ch), F32),
            pltpu.VMEM((2, rows, LANES), F32),
            pltpu.VMEM((2, n_a - 1, c_a, LANES), F32),
            pltpu.VMEM((2, c_a, LANES), F32),
            pltpu.VMEM((2, n_b - 1, c_b, LANES), F32),
            pltpu.VMEM((2, c_a, LANES), BF16),
            pltpu.VMEM((2, rows, LANES), BF16),
            dma((3, 2)), dma((3, 2)),
            dma((2, n_a + n_b)), dma((2, n_a + n_b)),
            dma((2, 2 * (n_a + n_b))), dma((2, 2 * (n_a + n_b))),
        ],
        compiler_params=pltpu.CompilerParams(
            collective_id=0, has_side_effects=True, vmem_limit_bytes=48 * 2**20),
    )(
        xd, mask.astype(F32), flat_kernel(conv_one), flat_kernel(conv_two),
        flat_flipped(conv_one), flat_flipped(conv_two), jnp.stack([gain, shift], axis=1),
    )
    shape = features.shape
    return (so.reshape(shape), ig.reshape(shape), g1.reshape(27, ch, ch),
            g2.reshape(27, ch, ch), gg.reshape(ch), sg.reshape(ch))


def solution(mesh):
    split = P("dp", None, "tile", None)
    return jax.shard_map(
        functools.partial(local, mesh.shape["dp"], mesh.shape["tile"]),
        mesh=mesh,
        in_specs=(split, P("dp", "tile", None), P(), P(), P(), P(), split),
        out_specs=(split, split, P(), P(), P(), P()),
        check_vma=False,
    )
```

profile of v0, /device:TPU:0, one launch (start us, length us, event | category | flops | bytes accessed | tf_op | source)
XLA Modules:
  0.0 62.7 jit_solution(9431107297689936470)
XLA Ops:
  0.7 0.6 %copy-done.4 = f32[64]{0:T(128)S(1)} copy-done((f32[64]{0:T(128)S(1)}, f32[64]{0:T(128)}, u32[]{:S(2)}) %copy-start.4) | copy-done | bytes 280
  1.3 0.6 %copy-done.6 = s32[1,1,2]{2,1,0:T(1,128)S(1)} copy-done((s32[1,1,2]{2,1,0:T(1,128)S(1)}, s32[1,1,2]{2,1,0:T(1,128)}, u32[]{:S(2)}) %copy-start.6) | copy-done | bytes 32
  2.0 0.1 copy.33.gs_ref
  2.1 0.1 broadcast_in_dim.8
  2.2 0.1 convert_element_type.31
  2.3 0.1 broadcast_in_dim.9
  2.3 0.1 convert_element_type.33.mask_ref
  2.5 1.2 %copy.28 = bf16[3,576,64]{1,2,0:T(8,128)(2,1)S(1)} copy(bf16[3,576,64]{2,1,0:T(8,128)(2,1)} %bitcast.51) | data formatting | bytes 442368 | tf_op jit(solution)/shard_map/reshape | solution.py:343
  3.7 0.2 copy.27
  4.0 0.7 %copy-done.2 = bf16[1,64,8,128]{3,2,1,0:T(8,128)(2,1)S(1)} copy-done((bf16[1,64,8,128]{3,2,1,0:T(8,128)(2,1)S(1)}, bf16[1,64,8,128]{3,2,1,0:T(8,128)(2,1)}, u32[]{:S(2)}) %copy-start.2) | copy-done | bytes 131096
  4.8 0.9 %copy.29 = bf16[3,9,64,64]{2,0,3,1:T(4,128)(2,1)S(1)} copy(bf16[3,9,64,64]{3,2,1,0:T(8,128)(2,1)S(1)} %bitcast.52) | data formatting | bytes 442368 | tf_op jit(solution)/shard_map/reshape | solution.py:348
  5.8 0.3 reshape.103
  6.1 0.2 copy.31.w1f_ref
  6.3 0.8 %copy-done.1 = bf16[27,64,64]{2,1,0:T(8,128)(2,1)S(1)} copy-done((bf16[27,64,64]{2,1,0:T(8,128)(2,1)S(1)}, bf16[27,64,64]{2,1,0:T(8,128)(2,1)}, u32[]{:S(2)}) %copy-start.1) | copy-done | bytes 221208
  7.2 0.9 %copy.30 = bf16[3,9,64,64]{2,0,3,1:T(4,128)(2,1)S(1)} copy(bf16[3,9,64,64]{3,2,1,0:T(8,128)(2,1)S(1)} %bitcast.53) | data formatting | bytes 442368 | tf_op jit(solution)/shard_map/reshape | solution.py:348
  8.1 0.3 reshape.105
  8.4 0.2 copy.32.w2f_ref
  8.6 49.9 %shard_map.118 = (bf16[64,1024]{1,0:T(8,128)(2,1)S(1)}, bf16[64,1024]{1,0:T(8,128)(2,1)S(1)}, f32[1728,64]{1,0:T(8,128)S(1)}, f32[1728,64]{1,0:T(8,128)S(1)}, f32[1,64]{1,0:T(1,128)S(1)}, /*index=5*/f32[1,64]{1,0:T(1,128)S(1)}) custom-call(bf16[128,1024]{1,0:T(8,128)(2,1)S(1)} %maximum_multiply_fusion.xd_ref, f32[1,1024]{1,0:T(1,128)S(1)} %convert_element_type.33.mask_ref, ...), custom_call_target="tpu_custom_call" | custom-call | tf_op jit(solution)/shard_map/pallas_call | solution.py:367
  58.5 0.7 %copy.36 = bf16[8,8,8,128]{3,2,1,0:T(8,128)(2,1)} copy(bf16[8,8,8,128]{3,1,2,0:T(8,128)(2,1)S(1)} %bitcast.45) | data formatting | bytes 262144
  59.2 0.7 %copy.37 = bf16[8,8,8,128]{3,2,1,0:T(8,128)(2,1)} copy(bf16[8,8,8,128]{3,1,2,0:T(8,128)(2,1)S(1)} %bitcast.44) | data formatting | bytes 262144
  59.9 0.9 %copy.44 = f32[27,64,64]{2,1,0:T(8,128)} copy(f32[27,64,64]{2,1,0:T(8,128)S(1)} %bitcast.43) | data formatting | bytes 884736
  60.8 0.9 %copy.45 = f32[27,64,64]{2,1,0:T(8,128)} copy(f32[27,64,64]{2,1,0:T(8,128)S(1)} %bitcast.42) | data formatting | bytes 884736
  61.7 0.5 copy.46
  62.2 0.5 copy.47
  (16 shorter events, 0.3 us)
Async XLA Ops:
  0.6 0.7 %copy-start.4 = (f32[64]{0:T(128)S(1)}, f32[64]{0:T(128)}, u32[]{:S(2)}) copy-start(f32[64]{0:T(128)} %param.12) | copy-start | bytes 772
  0.6 0.7 %copy-start.5 = (f32[64]{0:T(128)S(1)}, f32[64]{0:T(128)}, u32[]{:S(2)}) copy-start(f32[64]{0:T(128)} %param.11) | copy-start | bytes 772
  1.3 0.7 %copy-start.6 = (s32[1,1,2]{2,1,0:T(1,128)S(1)}, s32[1,1,2]{2,1,0:T(1,128)}, u32[]{:S(2)}) copy-start(s32[1,1,2]{2,1,0:T(1,128)} %param.8) | copy-start | bytes 28
  2.1 1.6 %copy-start = (bf16[27,64,64]{2,1,0:T(8,128)(2,1)S(1)}, bf16[27,64,64]{2,1,0:T(8,128)(2,1)}, u32[]{:S(2)}) copy-start(bf16[27,64,64]{2,1,0:T(8,128)(2,1)} %param.9) | copy-start | bytes 663556
  3.7 0.9 %copy-start.2 = (bf16[1,64,8,128]{3,2,1,0:T(8,128)(2,1)S(1)}, bf16[1,64,8,128]{3,2,1,0:T(8,128)(2,1)}, u32[]{:S(2)}) copy-start(bf16[1,64,8,128]{3,2,1,0:T(8,128)(2,1)} %param.13) | copy-start | bytes 393220
  3.7 1.0 %copy-start.3 = (bf16[1,64,8,128]{3,2,1,0:T(8,128)(2,1)S(1)}, bf16[1,64,8,128]{3,2,1,0:T(8,128)(2,1)}, u32[]{:S(2)}) copy-start(bf16[1,64,8,128]{3,2,1,0:T(8,128)(2,1)} %param.7) | copy-start | bytes 393220
  6.1 1.0 %copy-start.1 = (bf16[27,64,64]{2,1,0:T(8,128)(2,1)S(1)}, bf16[27,64,64]{2,1,0:T(8,128)(2,1)}, u32[]{:S(2)}) copy-start(bf16[27,64,64]{2,1,0:T(8,128)(2,1)} %param.10) | copy-start | bytes 663556
where the time goes:
time: 62.9 us; the launch traced here: 62.7 us
  Pallas kernels  49.9 us (79%)
  local copies, waits for them, and re-layouts  12 us (19%)
  between operations  0.75 us (1%)
    pallas_call x1, Pallas kernels, local(): pl.pallas_call(functools.partial(kernel, n_dp, n_tile, ch, nx, hy), out_s...  49.9 us
    unnamed x20, local copies, waits for them, and re-layouts  7.08 us
    reshape x2, local copies, waits for them, and re-layouts, flat_flipped(): taps[::-1].reshape(3, count // 3, outer, inner).transpose(0, 2, 1, 3)  1.86 us
    reshape x2, local copies, waits for them, and re-layouts, flat_kernel(): taps.reshape(3, count // 3 * inner, outer).transpose(0, 2, 1)  1.44 us

commit v1 on v0

--- a/solution.py
+++ b/solution.py
@@ -17,9 +17,9 @@
 
 def kernel(
     n_dp, n_tile, ch, nx, hy,
-    xd_ref, mask_ref, w1_ref, w2_ref, w1f_ref, w2f_ref, gs_ref,
-    so_ref, ig_ref, g1_ref, g2_ref, gain_out, shift_out,
-    xd_pad, a_pad, i_pad, s_x, s_t, d3, ar_a, ar_b, part, r1, acc, r2, q3, q4,
+    xd_ref, occ_ref, k1_ref, k2_ref, gain_ref, shift_ref,
+    so_ref, ig_ref, q4, sums_out,
+    w1_ref, w2_ref, w1f_ref, w2f_ref, xd_pad, a_pad, i_pad, s_x, s_t, d3, ar_a, ar_b, part, r1, acc, r2, q3,
     halo_s, halo_r, ar_s, ar_r, rs_s, rs_r,
 ):
     n_a, n_b = 2 * n_dp, n_tile // 2
@@ -53,6 +53,31 @@
     @pl.when(has_right)
     def _():
         pl.semaphore_signal(barrier, inc=1, device_id=(dp, tile + 1), device_id_type=MESH)
+
+    width = hy // BLK
+    spot = lax.broadcasted_iota(jnp.int32, (1, flat), 1)
+    block_x, block_y = spot // (hy * BLK), lax.rem(spot, width) // BLK
+    mask = jnp.zeros((1, flat), F32)
+    for bx in range(nx // BLK):
+        for by in range(width // BLK):
+            mask = jnp.where((block_x == bx) & (block_y == by),
+                             occ_ref[bx, by].astype(F32), mask)
+    xd_pad[:, pl.ds(hy, flat)] = (xd_ref[...].astype(F32) * mask).astype(BF16)
+    same = (lax.broadcasted_iota(jnp.int32, (ch, ch), 0)
+            == lax.broadcasted_iota(jnp.int32, (ch, ch), 1)).astype(BF16)
+
+    def as_matrix(taps, out):
+        for a in range(3):
+            out[pl.ds(a * ch, ch), :] = lax.dot_general(
+                same, taps[pl.ds(a * 9 * ch, 9 * ch), :], (((1,), (1,)), ((), ())),
+                preferred_element_type=F32).astype(BF16)
+
+    def as_flipped(taps, out):
+        for a in range(3):
+            out[pl.ds(a * ch, ch), :] = jnp.concatenate(
+                [taps[pl.ds((26 - 9 * a - k) * ch, ch), :] for k in range(9)], axis=1)
+
+    as_matrix(k1_ref, w1_ref)
 
     sides = has_left.astype(jnp.int32) + has_right.astype(jnp.int32)
     pl.semaphore_wait(barrier, n_a + n_b - 2 + sides)
@@ -99,14 +124,13 @@
         def _():
             pad[:, pl.ds(flat + hy, hy)] = jnp.zeros((pad.shape[0], hy), pad.dtype)
 
-    width = hy // BLK
     lane = lax.broadcasted_iota(jnp.int32, (1, hy), 1)
     row_h, row_y = lane // width, lax.rem(lane, width)
 
     def shifts(pad, first, out):
         def plane(x, carry):
             at = pl.ds(pl.multiple_of(x * hy, hy), hy)
-            values = pad[pl.ds(first, ch), at].astype(F32)
+            values = pad[pl.ds(first, ch), at]
             for b in range(3):
                 for c in range(3):
                     step = (b - 1) * width + (c - 1)
@@ -115,10 +139,10 @@
                         moved = pltpu.roll(values, (-step) % hy, 1)
                         fits = ((row_h + (b - 1) >= 0) & (row_h + (b - 1) < BLK)
                                 & (row_y + (c - 1) >= 0) & (row_y + (c - 1) < width))
-                        moved = jnp.where(fits, moved, 0.0)
+                        moved = jnp.where(fits, moved, jnp.zeros_like(moved))
                     out[pl.ds((3 * b + c) * ch, ch), at] = moved.astype(BF16)
             return carry
-        lax.fori_loop(0, nx + 2, plane, 0)
+        lax.fori_loop(0, nx + 2, plane, 0, unroll=True)
 
     def conv(weight, stack):
         grown = jnp.dot(weight[...], stack[...], preferred_element_type=F32)
@@ -255,24 +279,17 @@
         q4[g, mine, :] = q3[g]
         return copies
 
-    def write_grad(g, copies, out):
-        wait_all(copies)
-        rows = 9 * ch
-        half = rows // 2
-        for a in range(2):
-            out[pl.ds(a * rows, rows), :] = q4[g, pl.ds(0, rows), pl.ds(a * ch, ch)].astype(F32)
-        for side in range(2):
-            out[pl.ds(2 * rows + side * half, half), :] = (
-                q4[g, pl.ds(rows, half), pl.ds(side * ch, ch)].astype(F32))
-
-    mask = mask_ref[...]
-    end_xd = halo(0, xd_ref, 0, xd_pad)
-    xd_pad[:, pl.ds(hy, flat)] = xd_ref[...]
+    end_xd = halo(0, xd_pad, hy, xd_pad)
+    as_flipped(k2_ref, w2f_ref)
+    as_matrix(k2_ref, w2_ref)
+    as_flipped(k1_ref, w1f_ref)
+    gain_shift = to_columns(jnp.concatenate(
+        [gain_ref[...], shift_ref[...], jnp.zeros((6, ch), F32)], axis=0))
     zero_ends(xd_pad)
     zero_ends(a_pad)
     zero_ends(i_pad)
     d3[...] = jnp.zeros(d3.shape, d3.dtype)
-    put_d3(xd_ref[pl.ds(ch, ch), :])
+    put_d3(xd_pad[pl.ds(ch, ch), pl.ds(hy, flat)])
     used = 27 * ch // 2
     for g in range(2):
         part[g, pl.ds(used, part.shape[1] - used), :] = jnp.zeros(
@@ -295,7 +312,7 @@
     count = moments[:, 2:3]
     mean = moments[:, 0:1] / count
     inv_std = lax.rsqrt(moments[:, 1:2] / count + EPSILON)
-    gain, shift = gs_ref[:, 0:1], gs_ref[:, 1:2]
+    gain, shift = gain_shift[:, 0:1], gain_shift[:, 1:2]
     normal = (pre - mean) * inv_std
     pre_act = gain * normal + shift
     sg = 1.0 / (1.0 + jnp.exp(-pre_act))
@@ -311,8 +328,7 @@
     copies = small_next(1, copies, add)
     kernel_grad(s_t, 0)
     totals = small_end(1, copies, add)
-    shift_out[...] = totals[0:1]
-    gain_out[...] = totals[1:2]
+    sums_out[...] = totals
     totals = to_columns(totals)
     delta_one = (gain * inv_std * (
         z_grad - totals[:, 0:1] / count - normal * (totals[:, 1:2] / count)) * mask).astype(BF16)
@@ -323,60 +339,61 @@
     one = scatter_a(1)
     two = scatter_a(0)
     pre_two = conv(w2_ref, s_t)
-    so_ref[...] = ((xd_ref[pl.ds(0, ch), :].astype(F32) + pre_two) * mask).astype(BF16)
+    so_ref[...] = ((xd_pad[pl.ds(0, ch), pl.ds(hy, flat)].astype(F32) + pre_two) * mask).astype(BF16)
     one = scatter_b(1, one)
     end_delta()
     shifts(i_pad, 0, s_t)
     two = scatter_b(0, two)
     one = gather_b(1, one)
     back = conv(w1f_ref, s_t)
-    ig_ref[...] = ((xd_ref[pl.ds(ch, ch), :].astype(F32) + back) * mask).astype(BF16)
+    ig_ref[...] = ((xd_pad[pl.ds(ch, ch), pl.ds(hy, flat)].astype(F32) + back) * mask).astype(BF16)
     two = gather_b(0, two)
     one = gather_a(1, one)
     two = gather_a(0, two)
-    write_grad(1, one, g1_ref)
-    write_grad(0, two, g2_ref)
-
-
-def flat_kernel(taps):
-    count, inner, outer = taps.shape
-    return taps.reshape(3, count // 3 * inner, outer).transpose(0, 2, 1).reshape(3 * outer, -1)
-
-
-def flat_flipped(taps):
-    count, outer, inner = taps.shape
-    return (taps[::-1].reshape(3, count // 3, outer, inner).transpose(0, 2, 1, 3)
-            .reshape(3 * outer, -1))
+    wait_all(one)
+    wait_all(two)
+
+
+def unpack(ch, so_in, ig_in, q4, sums, so_ref, ig_ref, g1_ref, g2_ref, gain_ref, shift_ref):
+    rows = 9 * ch
+    half = rows // 2
+    for g, out in ((1, g1_ref), (0, g2_ref)):
+        for a in range(2):
+            out[pl.ds(a * rows, rows), :] = q4[g, pl.ds(0, rows), pl.ds(a * ch, ch)].astype(F32)
+        for side in range(2):
+            out[pl.ds(2 * rows + side * half, half), :] = (
+                q4[g, pl.ds(rows, half), pl.ds(side * ch, ch)].astype(F32))
+    so_ref[...] = so_in[...]
+    ig_ref[...] = ig_in[...]
+    shift_ref[...] = sums[0:1, :]
+    gain_ref[...] = sums[1:2, :]
 
 
 def local(n_dp, n_tile, features, occupied, conv_one, conv_two, gain, shift, cotangent):
     scenes, ch, nx, hy = features.shape
     flat = nx * hy
-    grown = jnp.broadcast_to(
-        occupied[:, :, None, None, :, None],
-        (1, nx // BLK, BLK, BLK, occupied.shape[2], BLK)).reshape(1, flat)
-    mask = grown.astype(BF16)
-    xd = jnp.concatenate(
-        [features.reshape(ch, flat), cotangent.reshape(ch, flat)], axis=0) * mask
+    xd = jnp.concatenate([features.reshape(ch, flat), cotangent.reshape(ch, flat)], axis=0)
     n_a, n_b = 2 * n_dp, n_tile // 2
     c_b = -(-(27 * ch // 2) // (n_a * n_b * 16)) * 16
     c_a = c_b * n_b
     rows = c_a * n_a
     vmem = pl.BlockSpec(memory_space=pltpu.VMEM)
     dma = pltpu.SemaphoreType.DMA
-    so, ig, g1, g2, gg, sg = pl.pallas_call(
+    so, ig, q4, sums = pl.pallas_call(
         functools.partial(kernel, n_dp, n_tile, ch, nx, hy),
         out_shape=(
             jax.ShapeDtypeStruct((ch, flat), BF16),
             jax.ShapeDtypeStruct((ch, flat), BF16),
-            jax.ShapeDtypeStruct((27 * ch, ch), F32),
-            jax.ShapeDtypeStruct((27 * ch, ch), F32),
-            jax.ShapeDtypeStruct((1, ch), F32),
-            jax.ShapeDtypeStruct((1, ch), F32),
+            jax.ShapeDtypeStruct((2, rows, LANES), BF16),
+            jax.ShapeDtypeStruct((8, ch), F32),
         ),
-        in_specs=[vmem] * 7,
-        out_specs=[vmem] * 6,
+        in_specs=[vmem, pl.BlockSpec(memory_space=pltpu.SMEM)] + [vmem] * 4,
+        out_specs=[vmem] * 4,
         scratch_shapes=[
+            pltpu.VMEM((3 * ch, 9 * ch), BF16),
+            pltpu.VMEM((3 * ch, 9 * ch), BF16),
+            pltpu.VMEM((3 * ch, 9 * ch), BF16),
+            pltpu.VMEM((3 * ch, 9 * ch), BF16),
             pltpu.VMEM((2 * ch, flat + 2 * hy), BF16),
             pltpu.VMEM((ch, flat + 2 * hy), BF16),
             pltpu.VMEM((ch, flat + 2 * hy), BF16),
@@ -390,7 +407,6 @@
             pltpu.VMEM((2, c_a, LANES), F32),
             pltpu.VMEM((2, n_b - 1, c_b, LANES), F32),
             pltpu.VMEM((2, c_a, LANES), BF16),
-            pltpu.VMEM((2, rows, LANES), BF16),
             dma((3, 2)), dma((3, 2)),
             dma((2, n_a + n_b)), dma((2, n_a + n_b)),
             dma((2, 2 * (n_a + n_b))), dma((2, 2 * (n_a + n_b))),
@@ -398,9 +414,24 @@
         compiler_params=pltpu.CompilerParams(
             collective_id=0, has_side_effects=True, vmem_limit_bytes=48 * 2**20),
     )(
-        xd, mask.astype(F32), flat_kernel(conv_one), flat_kernel(conv_two),
-        flat_flipped(conv_one), flat_flipped(conv_two), jnp.stack([gain, shift], axis=1),
+        xd, occupied[0], conv_one.reshape(27 * ch, ch), conv_two.reshape(27 * ch, ch),
+        gain.reshape(1, ch), shift.reshape(1, ch),
     )
+    planes = features.shape[1:]
+    so, ig, g1, g2, gg, sg = pl.pallas_call(
+        functools.partial(unpack, ch),
+        out_shape=(
+            jax.ShapeDtypeStruct(planes, BF16),
+            jax.ShapeDtypeStruct(planes, BF16),
+            jax.ShapeDtypeStruct((27 * ch, ch), F32),
+            jax.ShapeDtypeStruct((27 * ch, ch), F32),
+            jax.ShapeDtypeStruct((1, ch), F32),
+            jax.ShapeDtypeStruct((1, ch), F32),
+        ),
+        in_specs=[vmem] * 4,
+        out_specs=[vmem] * 6,
+        compiler_params=pltpu.CompilerParams(vmem_limit_bytes=16 * 2**20),
+    )(so.reshape(planes), ig.reshape(planes), q4, sums)
     shape = features.shape
     return (so.reshape(shape), ig.reshape(shape), g1.reshape(27, ch, ch),
             g2.reshape(27, ch, ch), gg.reshape(ch), sg.reshape(ch))

time: 62.9 us -> 53.3 us (0.85)
  local copies, waits for them, and re-layouts: 12 us -> 1.78 us
  Pallas kernels: 49.9 us -> 50.6 us
    unnamed x20 -> x12, local copies, waits for them, and re-layouts: 7.08 us -> 0.71 us
    reshape x8 -> x0, local copies, waits for them, and re-layouts: 4.35 us -> none  [the longest x2 1.86 us: flat_flipped(): taps[::-1].reshape(3, count // 3, outer, inner).transpose(0, 2, 1, 3)]
    pallas_call x0 -> x1, Pallas kernels: none -> 1.42 us  [local(): pl.pallas_call(functools.partial(unpack, ch), out_shape=(jax.ShapeDtypeSt...]
    reshape x1, local copies, waits for them, and re-layouts: 0.03 us -> 1.07 us  [local(): cotangent.reshape(ch, flat)]
    pallas_call x1, Pallas kernels: 49.9 us -> 49.2 us  [local(): pl.pallas_call(functools.partial(kernel, n_dp, n_tile, ch, nx, hy), out_s...]
where the time goes in v1:
time: 53.3 us; the launch traced here: 53.1 us
  Pallas kernels  50.6 us (95%)
  local copies, waits for them, and re-layouts  1.78 us (3%)
  between operations  0.72 us (1%)
    pallas_call x1, Pallas kernels, local(): pl.pallas_call(functools.partial(kernel, n_dp, n_tile, ch, nx, hy), out_s...  49.2 us
    pallas_call x1, Pallas kernels, local(): pl.pallas_call(functools.partial(unpack, ch), out_shape=(jax.ShapeDtypeSt...  1.42 us
    reshape x1, local copies, waits for them, and re-layouts, local(): cotangent.reshape(ch, flat)  1.07 us

profile of v1, /device:TPU:0, one launch (start us, length us, event | category | flops | bytes accessed | tf_op | source)
XLA Modules:
  0.0 53.1 jit_solution(10222145751986045506)
XLA Ops:
  0.6 0.0 copy-start
  0.6 0.0 copy-start.1
  0.7 1.1 %copy_bitcast_fusion = (bf16[64,1024]{1,0:T(8,128)(2,1)S(1)}, bf16[64,1024]{1,0:T(8,128)(2,1)S(1)}) fusion(bf16[8,8,8,128]{3,2,1,0:T(8,128)(2,1)} %bitcast.32, bf16[8,8,8,128]{3,2,1,0:T(8,128)(2,1)} %bitcast.33), kind=kLoop, calls=%fused_computation.1 | loop fusion | bytes 524288 | tf_op jit(solution)/shard_map/reshape | solution.py:375
  1.7 0.0 copy-start.2
  1.7 0.0 copy-start.3
  1.8 0.0 copy-start.4
  1.8 0.0 copy-done
  1.8 0.1 copy-done.1
  1.9 0.5 copy-done.2
  2.4 0.0 copy-done.3
  2.4 0.0 copy-done.4
  2.5 49.2 %shard_map.118 = (bf16[64,1024]{1,0:T(8,128)(2,1)S(1)}, bf16[64,1024]{1,0:T(8,128)(2,1)S(1)}, bf16[2,1024,128]{2,1,0:T(8,128)(2,1)S(1)}, f32[8,64]{1,0:T(8,128)S(1)}) custom-call(bf16[128,1024]{1,0:T(8,128)(2,1)S(1)} %pad_maximum_fusion.xd_ref, s32[1,2]{1,0:T(1,128)S(1)} %bitcast.29, bf16[1728,64]{1,0:T(8,128)(2,1)S(1)} %bitcast.25, ...), custom_call_target="tpu_custom_call" | custom-call | tf_op jit(solution)/shard_map/pallas_call | solution.py:382
  51.7 1.4 %shard_map.119 = (bf16[64,8,128]{2,1,0:T(8,128)(2,1)}, bf16[64,8,128]{2,1,0:T(8,128)(2,1)}, f32[1728,64]{1,0:T(8,128)}, f32[1728,64]{1,0:T(8,128)}, f32[1,64]{1,0:T(1,128)}, /*index=5*/f32[1,64]{1,0:T(1,128)}) custom-call(bf16[64,8,128]{2,1,0:T(8,128)(2,1)S(1)} %bitcast.23, bf16[64,8,128]{2,1,0:T(8,128)(2,1)S(1)} %bitcast.24, ...), custom_call_target="tpu_custom_call" | custom-call | tf_op jit(solution)/shard_map/pallas_call | solution.py:421
  (3 shorter events, 0.1 us)
Async XLA Ops:
  0.6 1.2 %copy-start = (bf16[27,64,64]{2,1,0:T(8,128)(2,1)S(1)}, bf16[27,64,64]{2,1,0:T(8,128)(2,1)}, u32[]{:S(2)}) copy-start(bf16[27,64,64]{2,1,0:T(8,128)(2,1)} %param.9) | copy-start | bytes 663556
  0.6 1.3 %copy-start.1 = (bf16[27,64,64]{2,1,0:T(8,128)(2,1)S(1)}, bf16[27,64,64]{2,1,0:T(8,128)(2,1)}, u32[]{:S(2)}) copy-start(bf16[27,64,64]{2,1,0:T(8,128)(2,1)} %param.10) | copy-start | bytes 663556
  1.7 0.7 %copy-start.2 = (s32[1,1,2]{2,1,0:T(1,128)S(1)}, s32[1,1,2]{2,1,0:T(1,128)}, u32[]{:S(2)}) copy-start(s32[1,1,2]{2,1,0:T(1,128)} %param.8) | copy-start | bytes 28
  1.7 0.7 %copy-start.3 = (f32[64]{0:T(128)S(1)}, f32[64]{0:T(128)}, u32[]{:S(2)}) copy-start(f32[64]{0:T(128)} %param.11) | copy-start | bytes 772
  1.8 0.7 %copy-start.4 = (f32[64]{0:T(128)S(1)}, f32[64]{0:T(128)}, u32[]{:S(2)}) copy-start(f32[64]{0:T(128)} %param.12) | copy-start | bytes 772

commit v2 on v1

--- a/solution.py
+++ b/solution.py
@@ -19,20 +19,20 @@
     n_dp, n_tile, ch, nx, hy,
     xd_ref, occ_ref, k1_ref, k2_ref, gain_ref, shift_ref,
     so_ref, ig_ref, q4, sums_out,
-    w1_ref, w2_ref, w1f_ref, w2f_ref, xd_pad, a_pad, i_pad, s_x, s_t, d3, ar_a, ar_b, part, r1, acc, r2, q3,
+    w1_ref, w2_ref, w1f_ref, w2f_ref, xd_pad, a_pad, i_pad, s_x, s_t, d3, ar_a, ar_b, part, rp, half_sum, r1, acc, r2, q3,
     halo_s, halo_r, ar_s, ar_r, rs_s, rs_r,
 ):
     n_a, n_b = 2 * n_dp, n_tile // 2
     dp, tile = lax.axis_index("dp"), lax.axis_index("tile")
     core, z = lax.rem(tile, 2), tile // 2
-    a_me = dp * 2 + core
+    a_me = core * n_dp + dp
     flat = nx * hy
     c_a = part.shape[1] // n_a
     c_b = c_a // n_b
 
     def peer_a(k):
         other = lax.rem(a_me + k, n_a)
-        return other, (other // 2, z * 2 + lax.rem(other, 2))
+        return other, (lax.rem(other, n_dp), z * 2 + other // n_dp)
 
     def peer_b(k):
         other = lax.rem(z + k, n_b)
@@ -127,9 +127,9 @@
     lane = lax.broadcasted_iota(jnp.int32, (1, hy), 1)
     row_h, row_y = lane // width, lax.rem(lane, width)
 
-    def shifts(pad, first, out):
+    def shifts(pad, first, out, inner=True, outer=True):
         def plane(x, carry):
-            at = pl.ds(pl.multiple_of(x * hy, hy), hy)
+            at = pl.ds(x * hy if isinstance(x, int) else pl.multiple_of(x * hy, hy), hy)
             values = pad[pl.ds(first, ch), at]
             for b in range(3):
                 for c in range(3):
@@ -142,7 +142,11 @@
                         moved = jnp.where(fits, moved, jnp.zeros_like(moved))
                     out[pl.ds((3 * b + c) * ch, ch), at] = moved.astype(BF16)
             return carry
-        lax.fori_loop(0, nx + 2, plane, 0, unroll=True)
+        if inner:
+            lax.fori_loop(1, nx + 1, plane, 0, unroll=True)
+        if outer:
+            plane(0, 0)
+            plane(nx + 1, 0)
 
     def conv(weight, stack):
         grown = jnp.dot(weight[...], stack[...], preferred_element_type=F32)
@@ -217,23 +221,37 @@
             spread_all = spread_all + row[2:3] * off * off
         return jnp.concatenate([sums, spread_all, count, jnp.zeros((5, ch), F32)], axis=0)
 
-    def scatter_a(g):
+    half_rows = part.shape[1] // 2
+
+    def scatter_core(g):
+        theirs = pl.ds(pl.multiple_of((1 - core) * half_rows, half_rows), half_rows)
+        copy = pltpu.make_async_remote_copy(
+            src_ref=part.at[g, theirs, :], dst_ref=rp.at[g],
+            send_sem=rs_s.at[g, 0], recv_sem=rs_r.at[g, 0],
+            device_id=(dp, z * 2 + 1 - core), device_id_type=MESH)
+        copy.start()
+        return [copy]
+
+    def scatter_a(g, copies):
+        wait_all(copies)
+        mine = pl.ds(pl.multiple_of(core * half_rows, half_rows), half_rows)
+        half_sum[g] = part[g, mine, :] + rp[g]
         copies = []
-        for k in range(1, n_a):
-            other, device = peer_a(k)
+        for k in range(1, n_dp):
+            other = lax.rem(dp + k, n_dp)
             copy = pltpu.make_async_remote_copy(
-                src_ref=part.at[g, pl.ds(pl.multiple_of(other * c_a, c_a), c_a), :],
+                src_ref=half_sum.at[g, pl.ds(pl.multiple_of(other * c_a, c_a), c_a), :],
                 dst_ref=r1.at[g, k - 1],
                 send_sem=rs_s.at[g, k], recv_sem=rs_r.at[g, k],
-                device_id=device, device_id_type=MESH)
+                device_id=(other, tile), device_id_type=MESH)
             copy.start()
             copies.append(copy)
         return copies
 
     def scatter_b(g, copies):
         wait_all(copies)
-        total = part[g, pl.ds(pl.multiple_of(a_me * c_a, c_a), c_a), :]
-        for k in range(1, n_a):
+        total = half_sum[g, pl.ds(pl.multiple_of(dp * c_a, c_a), c_a), :]
+        for k in range(1, n_dp):
             total = total + r1[g, k - 1]
         acc[g] = total
         copies = []
@@ -280,34 +298,33 @@
         return copies
 
     end_xd = halo(0, xd_pad, hy, xd_pad)
-    as_flipped(k2_ref, w2f_ref)
-    as_matrix(k2_ref, w2_ref)
-    as_flipped(k1_ref, w1f_ref)
-    gain_shift = to_columns(jnp.concatenate(
-        [gain_ref[...], shift_ref[...], jnp.zeros((6, ch), F32)], axis=0))
+    shifts(xd_pad, 0, s_x, outer=False)
     zero_ends(xd_pad)
     zero_ends(a_pad)
     zero_ends(i_pad)
+    end_xd()
+
+    shifts(xd_pad, 0, s_x, inner=False)
+    pre = conv(w1_ref, s_x)
+    count_here = jnp.sum(mask, axis=1, keepdims=True)
+    sums_here = jnp.sum(pre * mask, axis=1, keepdims=True)
+    off = (pre - sums_here / jnp.maximum(count_here, 1.0)) * mask
+    squares_here = jnp.sum(off * off, axis=1, keepdims=True)
+    copies = small_start(0, to_rows([sums_here, squares_here, count_here]))
+
+    shifts(xd_pad, ch, s_t)
+    as_flipped(k2_ref, w2f_ref)
+    act_grad = conv(w2f_ref, s_t)
+    gain_shift = to_columns(jnp.concatenate(
+        [gain_ref[...], shift_ref[...], jnp.zeros((6, ch), F32)], axis=0))
+
+    copies = small_next(0, copies, merge_moments)
     d3[...] = jnp.zeros(d3.shape, d3.dtype)
     put_d3(xd_pad[pl.ds(ch, ch), pl.ds(hy, flat)])
     used = 27 * ch // 2
     for g in range(2):
         part[g, pl.ds(used, part.shape[1] - used), :] = jnp.zeros(
             (part.shape[1] - used, LANES), F32)
-    end_xd()
-
-    shifts(xd_pad, 0, s_x)
-    pre = conv(w1_ref, s_x)
-    count_here = jnp.sum(mask, axis=1, keepdims=True)
-    sums_here = jnp.sum(pre * mask, axis=1, keepdims=True)
-    off = (pre - sums_here / jnp.maximum(count_here, 1.0)) * mask
-    squares_here = jnp.sum(off * off, axis=1, keepdims=True)
-    copies = small_start(0, to_rows([sums_here, squares_here, count_here]))
-
-    shifts(xd_pad, ch, s_t)
-    act_grad = conv(w2f_ref, s_t)
-
-    copies = small_next(0, copies, merge_moments)
     moments = to_columns(small_end(0, copies, merge_moments))
     count = moments[:, 2:3]
     mean = moments[:, 0:1] / count
@@ -323,10 +340,14 @@
     gain_here = jnp.sum(z_grad * normal, axis=1, keepdims=True)
     copies = small_start(1, to_rows([shift_here, gain_here]))
 
+    as_matrix(k2_ref, w2_ref)
+    as_flipped(k1_ref, w1f_ref)
+    shifts(a_pad, 0, s_t, outer=False)
     end_act()
-    shifts(a_pad, 0, s_t)
+    shifts(a_pad, 0, s_t, inner=False)
     copies = small_next(1, copies, add)
     kernel_grad(s_t, 0)
+    two = scatter_core(0)
     totals = small_end(1, copies, add)
     sums_out[...] = totals
     totals = to_columns(totals)
@@ -336,20 +357,22 @@
     end_delta = halo(2, i_pad, hy, i_pad)
     put_d3(delta_one)
     kernel_grad(s_x, 1)
-    one = scatter_a(1)
-    two = scatter_a(0)
+    one = scatter_core(1)
+    two = scatter_a(0, two)
     pre_two = conv(w2_ref, s_t)
     so_ref[...] = ((xd_pad[pl.ds(0, ch), pl.ds(hy, flat)].astype(F32) + pre_two) * mask).astype(BF16)
+    one = scatter_a(1, one)
+    two = scatter_b(0, two)
+    shifts(i_pad, 0, s_t, outer=False)
+    end_delta()
+    shifts(i_pad, 0, s_t, inner=False)
     one = scatter_b(1, one)
-    end_delta()
-    shifts(i_pad, 0, s_t)
-    two = scatter_b(0, two)
-    one = gather_b(1, one)
+    two = gather_b(0, two)
     back = conv(w1f_ref, s_t)
     ig_ref[...] = ((xd_pad[pl.ds(ch, ch), pl.ds(hy, flat)].astype(F32) + back) * mask).astype(BF16)
-    two = gather_b(0, two)
+    one = gather_b(1, one)
+    two = gather_a(0, two)
     one = gather_a(1, one)
-    two = gather_a(0, two)
     wait_all(one)
     wait_all(two)
 
@@ -403,7 +426,9 @@
             pltpu.VMEM((2, n_a, 8, ch), F32),
             pltpu.VMEM((2, n_b, 8, ch), F32),
             pltpu.VMEM((2, rows, LANES), F32),
-            pltpu.VMEM((2, n_a - 1, c_a, LANES), F32),
+            pltpu.VMEM((2, rows // 2, LANES), F32),
+            pltpu.VMEM((2, rows // 2, LANES), F32),
+            pltpu.VMEM((2, n_dp - 1, c_a, LANES), F32),
             pltpu.VMEM((2, c_a, LANES), F32),
             pltpu.VMEM((2, n_b - 1, c_b, LANES), F32),
             pltpu.VMEM((2, c_a, LANES), BF16),

time: 53.3 us -> 48.2 us (0.904)
  Pallas kernels: 50.6 us -> 45.5 us
    pallas_call x1, Pallas kernels: 49.2 us -> 44.1 us  [local(): pl.pallas_call(functools.partial(kernel, n_dp, n_tile, ch, nx, hy), out_s...]
where the time goes in v2:
time: 48.2 us; the launch traced here: 48 us
  Pallas kernels  45.5 us (94%)
  local copies, waits for them, and re-layouts  1.78 us (4%)
  between operations  0.72 us (1%)
    pallas_call x1, Pallas kernels, local(): pl.pallas_call(functools.partial(kernel, n_dp, n_tile, ch, nx, hy), out_s...  44.1 us
    pallas_call x1, Pallas kernels, local(): pl.pallas_call(functools.partial(unpack, ch), out_shape=(jax.ShapeDtypeSt...  1.42 us
    reshape x1, local copies, waits for them, and re-layouts, local(): cotangent.reshape(ch, flat)  1.07 us

profile of v2, /device:TPU:0, one launch (start us, length us, event | category | flops | bytes accessed | tf_op | source)
XLA Modules:
  0.0 48.0 jit_solution(12467413298868787347)
XLA Ops:
  0.6 0.0 copy-start
  0.6 0.0 copy-start.1
  0.7 1.1 %copy_bitcast_fusion = (bf16[64,1024]{1,0:T(8,128)(2,1)S(1)}, bf16[64,1024]{1,0:T(8,128)(2,1)S(1)}) fusion(bf16[8,8,8,128]{3,2,1,0:T(8,128)(2,1)} %bitcast.32, bf16[8,8,8,128]{3,2,1,0:T(8,128)(2,1)} %bitcast.33), kind=kLoop, calls=%fused_computation.1 | loop fusion | bytes 524288 | tf_op jit(solution)/shard_map/reshape | solution.py:398
  1.7 0.0 copy-start.2
  1.7 0.0 copy-start.3
  1.8 0.0 copy-start.4
  1.8 0.0 copy-done
  1.8 0.1 copy-done.1
  1.9 0.5 %copy-done.2 = s32[1,1,2]{2,1,0:T(1,128)S(1)} copy-done((s32[1,1,2]{2,1,0:T(1,128)S(1)}, s32[1,1,2]{2,1,0:T(1,128)}, u32[]{:S(2)}) %copy-start.2) | copy-done | bytes 32
  2.4 0.0 copy-done.3
  2.4 0.0 copy-done.4
  2.5 44.1 %shard_map.118 = (bf16[64,1024]{1,0:T(8,128)(2,1)S(1)}, bf16[64,1024]{1,0:T(8,128)(2,1)S(1)}, bf16[2,1024,128]{2,1,0:T(8,128)(2,1)S(1)}, f32[8,64]{1,0:T(8,128)S(1)}) custom-call(bf16[128,1024]{1,0:T(8,128)(2,1)S(1)} %pad_maximum_fusion.xd_ref, s32[1,2]{1,0:T(1,128)S(1)} %bitcast.29, bf16[1728,64]{1,0:T(8,128)(2,1)S(1)} %bitcast.25, ...), custom_call_target="tpu_custom_call" | custom-call | tf_op jit(solution)/shard_map/pallas_call | solution.py:405
  46.6 1.4 %shard_map.119 = (bf16[64,8,128]{2,1,0:T(8,128)(2,1)}, bf16[64,8,128]{2,1,0:T(8,128)(2,1)}, f32[1728,64]{1,0:T(8,128)}, f32[1728,64]{1,0:T(8,128)}, f32[1,64]{1,0:T(1,128)}, /*index=5*/f32[1,64]{1,0:T(1,128)}) custom-call(bf16[64,8,128]{2,1,0:T(8,128)(2,1)S(1)} %bitcast.23, bf16[64,8,128]{2,1,0:T(8,128)(2,1)S(1)} %bitcast.24, ...), custom_call_target="tpu_custom_call" | custom-call | tf_op jit(solution)/shard_map/pallas_call | solution.py:446
  (3 shorter events, 0.1 us)
Async XLA Ops:
  0.6 1.2 %copy-start = (bf16[27,64,64]{2,1,0:T(8,128)(2,1)S(1)}, bf16[27,64,64]{2,1,0:T(8,128)(2,1)}, u32[]{:S(2)}) copy-start(bf16[27,64,64]{2,1,0:T(8,128)(2,1)} %param.9) | copy-start | bytes 663556
  0.6 1.3 %copy-start.1 = (bf16[27,64,64]{2,1,0:T(8,128)(2,1)S(1)}, bf16[27,64,64]{2,1,0:T(8,128)(2,1)}, u32[]{:S(2)}) copy-start(bf16[27,64,64]{2,1,0:T(8,128)(2,1)} %param.10) | copy-start | bytes 663556
  1.7 0.7 %copy-start.2 = (s32[1,1,2]{2,1,0:T(1,128)S(1)}, s32[1,1,2]{2,1,0:T(1,128)}, u32[]{:S(2)}) copy-start(s32[1,1,2]{2,1,0:T(1,128)} %param.8) | copy-start | bytes 28
  1.7 0.7 %copy-start.3 = (f32[64]{0:T(128)S(1)}, f32[64]{0:T(128)}, u32[]{:S(2)}) copy-start(f32[64]{0:T(128)} %param.11) | copy-start | bytes 772
  1.8 0.7 %copy-start.4 = (f32[64]{0:T(128)S(1)}, f32[64]{0:T(128)}, u32[]{:S(2)}) copy-start(f32[64]{0:T(128)} %param.12) | copy-start | bytes 772
